TPU v7x, 32 devices: a whole 2x2x4 slice. The times are simulated.
32 devices in a mesh: dp: 4 (over y, core), fsdp: 8 (over z, x).
Axes of the slice: x: 2, y: 2, z: 4, core: 2. Of those that a mesh axis runs over, the one named last changes fastest.
Arguments:
- rows_in: bfloat16 [96, 320, 1024], P(('dp', 'fsdp')), may hold values from -6 to 6
- slot_row: int32 [192], P(('dp', 'fsdp')), may hold values from 0 to 11, as said below
- live_count: int32 [32], P(('dp', 'fsdp')), may hold values from 1 to 3, as said below
- slot_activation_gradient: bfloat16 [192, 320, 1024], P(('dp', 'fsdp')), may hold values from -6 to 6
- query_weight: bfloat16 [1024, 1024], P(('dp', 'fsdp')), may hold values from -0.1875 to 0.1875
- key_weight: bfloat16 [1024, 1024], P(('dp', 'fsdp')), may hold values from -0.1875 to 0.1875
- value_weight: bfloat16 [1024, 1024], P(('dp', 'fsdp')), may hold values from -0.1875 to 0.1875
- output_weight: bfloat16 [1024, 1024], P(('dp', 'fsdp')), may hold values from -1.5 to 1.5
- query_bias: bfloat16 [1024], P(('dp', 'fsdp')), may hold values from -3 to 3
- value_bias: bfloat16 [1024], P(('dp', 'fsdp')), may hold values from -3 to 3
- output_bias: bfloat16 [1024], P(('dp', 'fsdp')), may hold values from -3 to 3
- attn_gain: bfloat16 [1024], P(('dp', 'fsdp')), may hold values from 0.5 to 1.5
- attn_shift: bfloat16 [1024], P(('dp', 'fsdp')), may hold values from -3 to 3
- expand_weight: bfloat16 [1024, 4096], P(('dp', 'fsdp')), may hold values from -0.1875 to 0.1875
- up_bias: bfloat16 [4096], P(('dp', 'fsdp')), may hold values from -3 to 3
- down_weight: bfloat16 [4096, 1024], P(('dp', 'fsdp')), may hold values from -0.1875 to 0.1875
- down_bias: bfloat16 [1024], P(('dp', 'fsdp')), may hold values from -3 to 3
- ffn_gain: bfloat16 [1024], P(('dp', 'fsdp')), may hold values from 0.5 to 1.5
- ffn_shift: bfloat16 [1024], P(('dp', 'fsdp')), may hold values from -3 to 3
Outputs:
- slot_acts: bfloat16 [192, 320, 1024], P(('dp', 'fsdp'))
- input_grad: float32 [96, 320, 1024], P(('dp', 'fsdp'))
- query_weight_grad: float32 [1024, 1024], P(('dp', 'fsdp'))
- key_weight_grad: float32 [1024, 1024], P(('dp', 'fsdp'))
- value_weight_grad: float32 [1024, 1024], P(('dp', 'fsdp'))
- output_weight_grad: float32 [1024, 1024], P(('dp', 'fsdp'))
- query_bias_grad: float32 [1024], P(('dp', 'fsdp'))
- value_bias_grad: float32 [1024], P(('dp', 'fsdp'))
- output_bias_grad: float32 [1024], P(('dp', 'fsdp'))
- attn_gain_grad: float32 [1024], P(('dp', 'fsdp'))
- attn_shift_grad: float32 [1024], P(('dp', 'fsdp'))
- up_weight_grad: float32 [1024, 4096], P(('dp', 'fsdp'))
- up_bias_grad: float32 [4096], P(('dp', 'fsdp'))
- down_weight_grad: float32 [4096, 1024], P(('dp', 'fsdp'))
- down_bias_grad: float32 [1024], P(('dp', 'fsdp'))
- ffn_gain_grad: float32 [1024], P(('dp', 'fsdp'))
- ffn_shift_grad: float32 [1024], P(('dp', 'fsdp'))
Inputs may be any that keep to these rules, and one draw needn't show every extreme that they name: v = slot_row[s] names row v % 3 of the device with dp index v // 3 and the slot's own fsdp index. Only live rows are named, and every live row is named by at least one slot. Row i of a device is live when i < live_count of that device. In every group of devices that share an fsdp index some device has 3.
All inputs are finite; a program needn't handle non-finite values.
Results may differ from a plain program's by a relative error of at most 0.02.
Values may be sent and summed in bfloat16 or wider, within the bound.
A program may use at most 256 MiB of HBM per device.

v0:
```python
import math
from functools import partial

import jax
import jax.numpy as jnp
from jax import lax
from jax.experimental import pallas as pl
from jax.experimental.pallas import tpu as pltpu
from jax.sharding import PartitionSpec as P

HEADS = 16


EPSILON = 1e-05


MESH = pl.DeviceIdType.MESH
LANES = 128


def place(nz, nx):
    dp, fs = lax.axis_index("dp"), lax.axis_index("fsdp")
    y, core = dp // 2, lax.rem(dp, 2)
    z, x = fs // nx, lax.rem(fs, nx)
    return y, core, z, x


def device(y, core, z, x, nx):
    return (y * 2 + core, z * nx + x)


class Partners:
    def __init__(self, nz, nx):
        self.nz, self.nx = nz, nx
        self.y, self.core, self.z, self.x = place(nz, nx)
        y, core, z, x = self.y, self.core, self.z, self.x
        self.sibling = device(y, 1 - core, z, x, nx)
        self.across_x = device(y, core, z, 1 - x, nx)
        self.across_y = device(1 - y, core, z, x, nx)
        self.along_z = [device(y, core, lax.rem(z + k, nz), x, nx) for k in range(1, nz)]
        self.all = [self.sibling, self.across_x, self.across_y, *self.along_z]

    def meet(self):
        barrier = pltpu.get_barrier_semaphore()
        for other in self.all:
            pl.semaphore_signal(barrier, inc=1, device_id=other, device_id_type=MESH)
        pl.semaphore_wait(barrier, len(self.all))


def remote(src, dst, send, recv, to):
    return pltpu.make_async_remote_copy(
        src_ref=src, dst_ref=dst, send_sem=send, recv_sem=recv, device_id=to, device_id_type=MESH
    )


def added(*blocks):
    total = blocks[0].astype(jnp.float32)
    for block in blocks[1:]:
        total = total + block.astype(jnp.float32)
    return total


class Scatter:
    def __init__(self, at, parts, rc, r3a, r3b, r2, rz, rcz, rcx, rcy, send, recv):
        self.at, self.parts = at, parts
        self.rc, self.r3a, self.r3b, self.r2, self.rz = rc, r3a, r3b, r2, rz
        self.rcz, self.rcx, self.rcy = rcz, rcx, rcy
        self.send, self.recv = send, recv

    def copy(self, m, i, src, dst, to):
        return remote(src, dst, self.send.at[m, i], self.recv.at[m, i], to)

    def to_sibling(self, m, theirs):
        return self.copy(m, 0, theirs, self.rc.at[m], self.at.sibling)

    def landings(self, m):
        a, b, c, _ = self.parts[m]
        a, b, c = (pl.ds(0, part.size) for part in (a, b, c))
        return (
            self.r3a.at[m, :, :, :, a],
            self.r3b.at[m, :, :, :, b],
            self.rcz.at[m, :, :, :, :, c],
            self.rcx.at[m, :, :, c],
            self.rcy.at[m, :, c],
        )

    def firsts(self, m):
        at, rc, nz = self.at, self.rc, self.at.nz
        a, b, c, _ = self.parts[m]
        r3a, r3b, rcz, _, _ = self.landings(m)
        return [
            self.copy(m, 1, rc.at[m, :, :, 1 - at.x, :, a], r3a, at.across_x),
            self.copy(m, 2, rc.at[m, 1 - at.y, :, :, :, b], r3b, at.across_y),
        ] + [
            self.copy(
                m, 2 + k, rc.at[m, :, lax.rem(at.z + k, nz), :, :, c], rcz.at[k - 1], at.along_z[k - 1]
            )
            for k in range(1, nz)
        ]

    def seconds(self, m):
        at, nz = self.at, self.at.nz
        a, b, _, _ = self.parts[m]
        r3a, r3b, rcz, rcx, _ = self.landings(m)
        return [
            self.copy(m, nz + 2, r3a.at[1 - at.y], self.r2.at[m, :, :, a], at.across_y),
            self.copy(m, nz + 3, r3b.at[:, 1 - at.x], self.r2.at[m, :, :, b], at.across_x),
            self.copy(m, nz + 4, rcz.at[0, :, 1 - at.x], rcx, at.across_x),
        ]

    def thirds(self, m):
        at, nz = self.at, self.at.nz
        ab = self.parts[m][3]
        rcx, rcy = self.landings(m)[3:]
        return [
            self.copy(
                m,
                nz + 4 + k,
                self.r2.at[m, lax.rem(at.z + k, nz), :, ab],
                self.rz.at[m, k - 1, :, ab],
                at.along_z[k - 1],
            )
            for k in range(1, nz)
        ] + [self.copy(m, 2 * nz + 4, rcx.at[1 - at.y], rcy, at.across_y)]

    def start(self, m, theirs):
        self.to_sibling(m, theirs).start()

    def step1(self, m, own):
        rc = self.rc
        self.to_sibling(m, rc.at[m]).wait_recv()

        rc[m] = added(rc[m], own).astype(rc.dtype)
        self.to_sibling(m, rc.at[m]).wait_send()
        for copy in self.firsts(m):
            copy.start()

    def step2(self, m):
        at, rc = self.at, self.rc
        a, b, c, _ = self.parts[m]
        r3a, r3b, rcz, _, _ = self.landings(m)
        for copy in self.firsts(m):
            copy.wait_recv()

        r3a[...] = added(r3a[...], rc[m, :, :, at.x, :, a]).astype(rc.dtype)
        r3b[...] = added(r3b[...], rc[m, at.y, :, :, :, b]).astype(rc.dtype)
        others = [rcz[k] for k in range(at.nz - 1)]
        rcz[0] = added(rc[m, :, at.z, :, :, c], *others).astype(rc.dtype)
        for copy in self.seconds(m):
            copy.start()

    def step3(self, m):
        at, r2 = self.at, self.r2
        a, b, _, _ = self.parts[m]
        r3a, r3b, rcz, rcx, _ = self.landings(m)
        for copy in self.seconds(m):
            copy.wait_recv()

        r2[m, :, :, a] = added(r2[m, :, :, a], r3a[at.y]).astype(r2.dtype)
        r2[m, :, :, b] = added(r2[m, :, :, b], r3b[:, at.x]).astype(r2.dtype)
        rcx[...] = added(rcx[...], rcz[0, :, at.x]).astype(r2.dtype)
        for copy in self.thirds(m):
            copy.start()

    def step4(self, m, out):
        at = self.at
        _, _, c, ab = self.parts[m]
        rcx, rcy = self.landings(m)[3:]
        for copy in self.thirds(m):
            copy.wait_recv()
        others = [self.rz[m, k, :, ab] for k in range(at.nz - 1)]
        out[m, :, ab] = added(self.r2[m, at.z, :, ab], *others)
        out[m, :, c] = added(rcx[at.y], rcy[...])

    def drain(self, m):
        for copy in self.firsts(m) + self.seconds(m) + self.thirds(m):
            copy.wait_send()


class SmallSum:
    def __init__(self, at, total, landing, send, recv):
        self.at, self.total, self.landing, self.send, self.recv = at, total, landing, send, recv

    def hop(self, i, to):
        return remote(self.total.at[i], self.landing.at[i], self.send.at[i], self.recv.at[i], to)

    def along(self, k):
        i = 2 + k
        return remote(self.total.at[3], self.landing.at[i], self.send.at[i], self.recv.at[i], self.at.along_z[k - 1])

    def start(self):
        self.hop(0, self.at.sibling).start()

    def step(self, i):
        at = self.at
        to = (at.sibling, at.across_x, at.across_y)
        self.hop(i, to[i]).wait_recv()
        self.total[i + 1] = self.total[i] + self.landing[i]
        if i < 2:
            self.hop(i + 1, to[i + 1]).start()
        else:
            for k in range(1, at.nz):
                self.along(k).start()

    def finish(self, out):
        at = self.at
        for k in range(1, at.nz):
            self.along(k).wait_recv()
        total = self.total[3]
        for k in range(1, at.nz):
            total = total + self.landing[2 + k]
        out[...] = total
        to = (at.sibling, at.across_x, at.across_y)
        for i in range(3):
            self.hop(i, to[i]).wait_send()
        for k in range(1, at.nz):
            self.along(k).wait_send()


def scatter_scratch(count, nz, nx, rows, columns, parts):
    bf16 = jnp.bfloat16
    a, b, c, ab = (max(part[i].size for part in parts) for i in range(4))
    return [
        pltpu.VMEM((count, 2, nz, nx, rows, columns), bf16),
        pltpu.VMEM((count, 2, nz, rows, a), bf16),
        pltpu.VMEM((count, nz, nx, rows, b), bf16),
        pltpu.VMEM((count, nz, rows, ab), bf16),
        pltpu.VMEM((count, nz - 1, rows, ab), bf16),
        pltpu.VMEM((count, nz - 1, 2, nx, rows, c), bf16),
        pltpu.VMEM((count, 2, rows, c), bf16),
        pltpu.VMEM((count, rows, c), bf16),
        pltpu.SemaphoreType.DMA((count, 2 * nz + 5)),
        pltpu.SemaphoreType.DMA((count, 2 * nz + 5)),
    ]


def small_scratch(nz, shape):
    return [
        pltpu.VMEM((4, *shape), jnp.float32),
        pltpu.VMEM((2 + nz, *shape), jnp.float32),
        pltpu.SemaphoreType.DMA((2 + nz,)),
        pltpu.SemaphoreType.DMA((2 + nz,)),
    ]


GATHER_SHARES = [
    (6, 1), (4, 2), (6, 1), (3, 4), (6, 1), (4, 3), (3, 4), (5, 1), (5, 1), (6, 1), (4, 2), (5, 1),
]
SCATTER_SHARES = [
    (5, 1), (4, 2), (6, 1), (4, 2), (4, 2), (4, 2), (5, 2), (6, 1), (6, 1), (5, 2), (4, 3), (3, 3),
]

FORWARD_ORDER = (
    100, 101, 102, 103, 0, 0, 104, 105, 0, 0, 0, 0, 200, 0, 201, 500, 300, 202, 301, 203, 302, 204, 205, 501,
    303, 400, 106, 0, 401, 107, 502, 304, 0, 402, 108, 305, 0, 403, 109, 503, 0, 206, 0, 0, 504, 0, 207, 0, 0,
    0, 404, 110, 0, 505, 0, 0, 208, 0, 306, 0, 405, 111, 0, 307, 0, 209, 0, 308, 210, 0, 406, 211, 0, 309, 407,
    506, 310, 0, 311, 408, 507, 0, 409, 508, 509, 410, 0, 510, 0, 411, 511, 0, 0,
)
BACKWARD_ORDER = (
    500, 0, 501, 0, 502, 0, 0, 503, 0, 100, 0, 0, 101, 0, 0, 504, 102, 0, 0, 103, 200, 0, 0, 0, 201, 104, 0, 0,
    505, 0, 0, 202, 105, 0, 203, 0, 300, 0, 301, 0, 106, 0, 204, 302, 0, 506, 0, 400, 0, 107, 205, 401, 303, 0,
    507, 0, 0, 508, 0, 206, 108, 402, 304, 0, 0, 0, 509, 0, 0, 403, 0, 207, 0, 305, 0, 306, 0, 510, 0, 404, 0,
    511, 0, 0, 0, 405, 208, 307, 0, 109, 0, 406, 0, 110, 0, 0, 111, 308, 407, 0, 209, 0, 210, 211, 309, 310,
    408, 311, 409, 410, 411,
)


def drive(order, items, run):
    todo = list(order)
    for item in items:
        while todo[0]:
            run(todo.pop(0))
        if callable(item):
            todo.pop(0)
            item()
            continue
        rounds, body = item
        between = []
        for _ in range(rounds):
            codes = []
            while todo[0]:
                codes.append(todo.pop(0))
            todo.pop(0)
            between.append(codes)

        def one(i, carry):
            for r, codes in enumerate(between):
                if codes:

                    @pl.when(i == r)
                    def _(codes=codes):
                        for code in codes:
                            run(code)

            body(i)
            return carry

        lax.fori_loop(0, rounds, one, 0)
    for code in todo:
        run(code)


def exact_gelu(pre):
    half = 0.5 + 0.5 * lax.erf(pre * (0.5**0.5))
    bell = jnp.exp(-0.5 * pre * pre) * ((0.5 / math.pi) ** 0.5)
    return pre * half, half + pre * bell


def rms_center(hidden):
    center = hidden - jnp.mean(hidden, axis=-1, keepdims=True)
    inverse = lax.rsqrt(jnp.mean(center * center, axis=-1, keepdims=True) + EPSILON)
    return center * inverse, inverse


def half_masks(width):
    left = (lax.broadcasted_iota(jnp.int32, (1, width), 1) < width // 2).astype(jnp.float32)
    return left.astype(jnp.bfloat16), (1.0 - left).astype(jnp.bfloat16)


def across(left, right):
    return lax.dot_general(left, right, (((1,), (1,)), ((), ())), preferred_element_type=jnp.float32)


def down(left, right):
    return lax.dot_general(left, right, (((0,), (0,)), ((), ())), preferred_element_type=jnp.float32)


def dot(left, right):
    return jnp.dot(left, right, preferred_element_type=jnp.float32)


def span(i, size):
    return pl.ds(pl.multiple_of(i * size, size), size)


class Gather:
    def __init__(self, at, parts, count, shards, g, send, recv):
        self.at, self.count, self.shards, self.g, self.send, self.recv = at, count, shards, g, send, recv
        self.parts = parts

    def copy(self, m, i, src, dst, to):
        return remote(src, dst, self.send.at[m, i], self.recv.at[m, i], to)

    def same(self, m, i, part, to):
        return self.copy(m, i, part, part, to)

    def stages(self, m):
        at, g, nz = self.at, self.g, self.at.nz
        a, b, c, ab = self.parts[m]
        y, core, z, x = at.y, at.core, at.z, at.x
        across_x, across_y, along_z = at.across_x, at.across_y, at.along_z
        first = [
            self.copy(m, k, self.shards.at[m, :, ab], g.at[m, y, core, z, x, :, ab], along_z[k])
            for k in range(nz - 1)
        ]
        first.append(self.copy(m, nz - 1, self.shards.at[m, :, c], g.at[m, y, core, z, x, :, c], across_y))
        second = [
            self.same(m, nz, g.at[m, y, core, :, x, :, a], across_y),
            self.same(m, nz + 1, g.at[m, y, core, :, x, :, b], across_x),
            self.same(m, nz + 2, g.at[m, :, core, z, x, :, c], across_x),
        ]
        third = [
            self.same(m, nz + 3, g.at[m, :, core, :, x, :, a], across_x),
            self.same(m, nz + 4, g.at[m, y, core, :, :, :, b], across_y),
        ]
        third += [self.same(m, nz + 5 + k, g.at[m, :, core, z, :, :, c], along_z[k]) for k in range(nz - 1)]
        return first, second, third, [self.same(m, 2 * nz + 4, g.at[m, :, core], at.sibling)]

    def step0(self, m):
        at = self.at
        for copy in self.stages(m)[0]:
            copy.start()
        self.g[m, at.y, at.core, at.z, at.x] = self.shards[m]

    def follow(self, stage, m):
        stages = self.stages(m)
        for copy in stages[stage - 1]:
            copy.wait_recv()
        for copy in stages[stage]:
            copy.start()

    def step1(self, m):
        self.follow(1, m)

    def step2(self, m):
        self.follow(2, m)

    def step3(self, m):
        self.follow(3, m)

    def arrive(self, m):
        part = self.g.at[m, :, self.at.core]
        self.same(m, 2 * self.at.nz + 4, part, self.at.sibling).wait_recv()

    def drain(self, m):
        for stage in self.stages(m):
            for copy in stage:
                copy.wait_send()


def column_parts(width, shares):
    lanes = 128
    a, b = (share * lanes for share in shares)
    return pl.ds(0, a), pl.ds(a, b), pl.ds(a + b, width - a - b), pl.ds(0, a + b)


UP_TILE = 256
NORM_ROWS = 192


def forward_kernel(
    nz, nx, parts, tokens, head_pair,
    x, attention_weights, expand, contract, small, slot_row, slots,
    g_out, probs_out, saved, act_out, slope_out, unit_out, final_out, own_out, across_out, small_full, inverse1, inverse2,
    g, shards, pool, hidden, landed, total, landing,
    send, recv, ssend, srecv, usend, urecv, across_send, across_recv, isem, gsem, vsem, asem, dsem, fsem, held_probs, ksem,
):
    f32, bf16 = jnp.float32, jnp.bfloat16
    count = g.shape[0]
    all_rows, width = x.shape
    rows = all_rows // tokens
    at = Partners(nz, nx)
    at.meet()
    gather = Gather(at, parts, count, shards, g, send, recv)
    sums = SmallSum(at, total, landing, ssend, srecv)
    groups = slots.shape[0] // rows

    def fetch(i):
        return pltpu.make_async_copy(slots.at[i], pool.at[i // rows, pl.ds((i % rows) * tokens, tokens)], isem.at[i])

    shard = shards.shape[1]
    lane = lax.broadcasted_iota(jnp.int32, (1, width), 1)
    mine = lane // shard == lax.axis_index("dp") * (nz * nx) + lax.axis_index("fsdp")
    own = [ref[...].astype(f32).reshape(1, -1) for ref in small]
    own = own[:-1] + [own[-1][:, i : i + shard] for i in range(0, own[-1].shape[1], shard)]
    own += [jnp.zeros((1, shard), f32)] * (total.shape[1] - len(own))
    own = jnp.concatenate(own, axis=0)
    total[0] = jnp.where(mine, jnp.concatenate([own] * (width // shard), axis=1), 0.0)
    sums.start()
    for m in range(4):
        shards[m] = attention_weights[m][...]
    for i in range(slots.shape[0]):
        fetch(i).start()

    high, part = 32, width // 2

    chosen = [
        [jnp.where(slot_row[s] == t, 1.0, 0.0) for s in range(slots.shape[0])] for t in range(2 * 2 * rows)
    ]

    def sum_slots(i, carry):
        cols = span(lax.rem(i, 2), part)
        base = i // 2 * high
        held = [
            pool[s // rows, pl.ds(pl.multiple_of(base + (s % rows) * tokens, high), high), cols].astype(f32)
            for s in range(slots.shape[0])
        ]
        for t in range(2 * 2 * rows):
            picked = chosen[t][0] * held[0]
            for s in range(1, slots.shape[0]):
                picked = picked + chosen[t][s] * held[s]
            spot = pl.ds(pl.multiple_of(base + (t % rows) * tokens, high), high)
            pool[groups + t // rows, spot, cols] = picked.astype(bf16)
        return carry

    def up_sibling(y):
        src = pool.at[groups + y * 2 + 1 - at.core]
        return remote(src, landed.at[y], usend.at[y], urecv.at[y], at.sibling)

    pieces = across_send.shape[0]

    def up_across(i):
        piece = pl.ds(i * (all_rows // pieces), all_rows // pieces)
        return remote(
            landed.at[1 - at.y, piece], across_out.at[piece], across_send.at[i], across_recv.at[i], at.across_y
        )

    up_own = pltpu.make_async_copy(landed.at[at.y], own_out, isem.at[slots.shape[0]])

    steps = tokens // high * 2

    def quarter(i):
        if i == 0:
            for s in range(slots.shape[0]):
                fetch(s).wait()
        lax.fori_loop(i * steps // 4, (i + 1) * steps // 4, sum_slots, 0)
        if i != 2:
            sums.step((0, 1, None, 2)[i])

    blocks = (count - 4) // 2

    def arrange():
        for j in range(blocks):
            shards[5 + 2 * j] = contract[j * shard : (j + 1) * shard, :]
        lanes = 128
        per = lanes // shard
        for q in range(width // lanes):
            natural = expand[:, q * lanes * blocks : (q + 1) * lanes * blocks].astype(f32)
            for j in range(blocks):
                starts = [t * blocks * shard + j * shard for t in range(per)]
                found = [natural[:, start : start + shard] for start in starts]
                shards[4 + 2 * j, :, q * lanes : (q + 1) * lanes] = jnp.concatenate(found, axis=1).astype(bf16)

    def exchange_cores():
        for y in range(2):
            up_sibling(y).start()

    def chip_sum(i, carry):
        y, spot = i // (all_rows // 192), span(lax.rem(i, all_rows // 192), 192)
        landed[y, spot] = added(landed[y, spot], pool[groups + y * 2 + at.core, spot]).astype(bf16)
        return carry

    def sum_chip():
        for y in range(2):
            up_sibling(y).wait_recv()
        lax.fori_loop(0, 2 * all_rows // 192, chip_sum, 0)
        up_own.start()
        for y in range(2):
            up_sibling(y).wait_send()

    def keep(m):
        return pltpu.make_async_copy(g.at[m], g_out.at[m], gsem.at[m])

    def arrive(m):
        gather.arrive(m)
        keep(m).start()

    def tile(m, cols):
        return g[m, :, :, :, :, :, cols].reshape(width, cols.size)

    def bias(i, cols):
        return small_full[pl.ds(i, 1), cols]

    every = pl.ds(0, all_rows)
    halves = [pl.ds(i * width // 2, width // 2) for i in range(2)]

    def tiles(size, body):
        def one(i, carry):
            body(span(i, size), every)
            return carry

        lax.fori_loop(0, width // size, one, 0)

    def save(i):
        return pltpu.make_async_copy(pool.at[i], saved.at[i], vsem.at[i])

    def project(m):
        row = lax.rem(m, 2) * 12 + m // 2
        arrive(m)
        pl.when(m == 0)(lambda: sums.finish(small_full))
        for cols in halves:
            pool[m, :, cols] = (dot(x[...], tile(m, cols)) + bias(row, cols)).astype(bf16)
        save(m).start()

    pairs = width // head_pair
    masks = half_masks(head_pair)
    scale = (head_pair // 2) ** (-0.5)

    def keep_probs(i):
        slot = lax.rem(i, 2)
        return pltpu.make_async_copy(held_probs.at[slot], probs_out.at[i], ksem.at[slot])

    def attend(i):
        spot, base = span(i // (pairs // 2), tokens), lax.rem(i, pairs // 2) * 2
        pl.when(i >= 2)(lambda: keep_probs(i - 2).wait())
        for p in range(2):
            cols = span(base + p, head_pair)
            query, keys, values = pool[0, spot, cols], pool[1, spot, cols], pool[2, spot, cols]
            query = query * jnp.asarray(scale, bf16)
            out = None
            for h, mask in enumerate(masks):
                scores = across(keys * mask, query)
                probs = jnp.exp(scores - jnp.max(scores, axis=0, keepdims=True))
                probs = (probs * (1.0 / jnp.sum(probs, axis=0, keepdims=True))).astype(bf16)
                held_probs[lax.rem(i, 2), 2 * p + h] = probs
                term = down(probs, values * mask)
                out = term if out is None else out + term
            pool[3, spot, cols] = out.astype(bf16)
        keep_probs(i).start()

    rounds = rows * pairs // 2

    def mix(cols, spot):
        hidden[spot, cols] = dot(pool[3, spot], tile(3, cols)) + x[spot, cols].astype(f32) + bias(2, cols)

    def join():
        save(3).start()
        for i in range(2):
            keep_probs(rounds - 2 + i).wait()
        arrive(3)
        for cols in halves:
            mix(cols, every)

    def unit(i):
        return pltpu.make_async_copy(pool.at[6], unit_out.at[i], fsem.at[i])

    def norm1(i, carry):
        spot = span(i, NORM_ROWS)
        normed, inverse = rms_center(hidden[spot])
        result = normed * small_full[3:4, :] + small_full[4:5, :]
        hidden[spot] = result
        pool[4, spot] = result.astype(bf16)
        pool[6, spot] = normed.astype(bf16)
        inverse1[spot] = inverse
        return carry

    def first_norm():
        lax.fori_loop(0, all_rows // NORM_ROWS, norm1, 0)
        save(4).start()
        unit(0).start()

    def save_act(j):
        return pltpu.make_async_copy(pool.at[5], act_out.at[j], asem)

    def save_slope(j):
        return pltpu.make_async_copy(pool.at[6], slope_out.at[j], dsem)

    def widen(j):
        pl.when(j == 0)(lambda: unit(0).wait())

        @pl.when(j > 0)
        def _():
            save_act(j - 1).wait()
            save_slope(j - 1).wait()

        def up(cols, spot):
            value, slope = exact_gelu(dot(pool[4, spot], tile(4 + 2 * j, cols)) + bias(8 + j, cols))
            pool[5, spot, cols] = value.astype(bf16)
            pool[6, spot, cols] = slope.astype(bf16)

        tiles(UP_TILE, up)
        save_act(j).start()
        save_slope(j).start()

    def narrow(j):
        for cols in halves:
            hidden[:, cols] = hidden[:, cols] + dot(pool[5], tile(5 + 2 * j, cols))

    def feed(i):
        arrive(4 + i)
        pl.when(lax.rem(i, 2) == 0)(lambda: widen(i // 2))
        pl.when(lax.rem(i, 2) == 1)(lambda: narrow(i // 2))

    def norm2(i, carry):
        spot = span(i, NORM_ROWS)
        normed, inverse = rms_center(hidden[spot] + small_full[5:6, :])
        pool[5, spot] = (normed * small_full[6:7, :] + small_full[7:8, :]).astype(bf16)
        pool[6, spot] = normed.astype(bf16)
        inverse2[spot] = inverse
        return carry

    finish = pltpu.make_async_copy(pool.at[5], final_out, fsem.at[2])

    def second_norm():
        save_act(blocks - 1).wait()
        save_slope(blocks - 1).wait()
        lax.fori_loop(0, all_rows // NORM_ROWS, norm2, 0)
        finish.start()
        unit(1).start()

    def run(code):
        kind, m = divmod(code, 100)
        if kind == 5:
            up_across(m).start()
        else:
            (gather.step0, gather.step1, gather.step2, gather.step3)[kind - 1](m)

    items = [partial(quarter, 0), arrange, *(partial(quarter, i) for i in (1, 2, 3)), exchange_cores, sum_chip]
    items += [(3, project), (rounds, attend), join, first_norm, (2 * blocks, feed), second_norm]
    drive(FORWARD_ORDER, items, run)
    for m in range(count):
        gather.drain(m)
        keep(m).wait()
    for i in range(5):
        save(i).wait()
    up_own.wait()
    for i in range(pieces):
        up_across(i).wait()
    finish.wait()
    unit(1).wait()


def forward(x, attention_weights, expand, contract, small, slot_row, slots, nz, nx, tokens):
    f32, bf16 = jnp.float32, jnp.bfloat16
    shard_rows, width = attention_weights[0].shape
    count = 4 + 2 * contract.shape[0] // shard_rows
    small_shape = (16, width)
    all_rows = x.shape[0]
    assert slots.shape[0] * tokens == 2 * all_rows
    vmem, anywhere = pl.BlockSpec(memory_space=pltpu.VMEM), pl.BlockSpec(memory_space=pl.ANY)
    acts = (all_rows, width)
    rows = all_rows // tokens
    blocks = (count - 4) // 2
    dma = pltpu.SemaphoreType.DMA
    full = (count, 2, 2, nz, nx, shard_rows, width)
    out = jax.ShapeDtypeStruct
    return pl.pallas_call(
        partial(forward_kernel, nz, nx, [column_parts(width, s) for s in GATHER_SHARES], tokens, 2 * width // HEADS),
        out_shape=[
            out(full, bf16),
            out((rows * HEADS // 4, 4, tokens, tokens), bf16),
            out((5, *acts), bf16),
            out((blocks, *acts), bf16),
            out((blocks, *acts), bf16),
            out((2, *acts), bf16),
            out(acts, bf16),
            out(acts, bf16),
            out(acts, bf16),
            out(small_shape, f32),
            out((all_rows, 1), f32),
            out((all_rows, 1), f32),
        ],
        in_specs=[vmem, [vmem] * 4, vmem, vmem, [vmem] * len(small), pl.BlockSpec(memory_space=pltpu.SMEM), anywhere],
        out_specs=[anywhere] * 9 + [vmem] * 3,
        scratch_shapes=[
            pltpu.VMEM(full, bf16),
            pltpu.VMEM((count, shard_rows, width), bf16),
            pltpu.VMEM((7, *acts), bf16),
            pltpu.VMEM(acts, f32),
            pltpu.VMEM((2, *acts), bf16),
            *small_scratch(nz, small_shape)[:2],
            dma((count, 2 * nz + 5)),
            dma((count, 2 * nz + 5)),
            dma((2 + nz,)),
            dma((2 + nz,)),
            dma((2,)),
            dma((2,)),
            dma((count,)),
            dma((count,)),
            dma((slots.shape[0] + 1,)),
            dma((count,)),
            dma((5,)),
            dma,
            dma,
            dma((3,)),
            pltpu.VMEM((2, 4, tokens, tokens), bf16),
            dma((2,)),
        ],
        compiler_params=pltpu.CompilerParams(
            collective_id=1, has_side_effects=True, vmem_limit_bytes=60 * 2**20
        ),
    )(x, attention_weights, expand, contract, small, slot_row, slots)


def quietly(call):
    call()


def backward_kernel(
    nz, nx, parts, tokens, head_pair,
    x, own_up, across_up, final, unit, inverse1, inverse2, small_full, act, slope, saved, g, probs,
    out, small_out, input_out, table,
    rc, r3a, r3b, r2, rz, rcz, rcx, rcy, send, recv, total, landing, ssend, srecv,
    term, weight, pool, hidden, wsem, psem, hsem, tsend, trecv, across_send, across_recv, tsem, held_probs, ksem,
):
    f32, bf16 = jnp.float32, jnp.bfloat16
    count = out.shape[0]
    all_rows, width = x.shape
    rows = all_rows // tokens
    at = Partners(nz, nx)
    at.meet()
    scatter = Scatter(at, parts, rc, r3a, r3b, r2, rz, rcz, rcx, rcy, send, recv)
    sums = SmallSum(at, total, landing, ssend, srecv)

    here = pltpu.make_async_copy(final, table.at[at.y, at.core], tsem)
    to_sibling = remote(final, table.at[at.y, at.core], tsend.at[0], trecv.at[0], at.sibling)
    pieces = across_send.shape[0]

    def to_across(i):
        piece = pl.ds(i * (all_rows // pieces), all_rows // pieces)
        dst = table.at[at.y, at.core, piece]
        return remote(final.at[piece], dst, across_send.at[i], across_recv.at[i], at.across_y)

    passed = table.at[1 - at.y, at.core]
    pass_on = remote(passed, passed, tsend.at[1], trecv.at[1], at.sibling)

    def load(src, entry, i):
        return pltpu.make_async_copy(src, pool.at[entry], psem.at[i])

    def fetch(m, slot, i):
        return pltpu.make_async_copy(g.at[m], weight.at[slot], wsem.at[i])

    blocks = act.shape[0]
    up_block, down_block = (lambda j: 4 + 2 * j), (lambda j: 5 + 2 * j)
    unit2, own_load, across_load = load(unit.at[1], 1, 0), load(own_up, 2, 1), load(across_up, 3, 2)
    act_entry = [5, 2, 3, 5]
    act_load = [load(act.at[j], act_entry[j], 3 + j) for j in range(blocks)]
    slope_entry = [4, 2, 3, 4]
    slope_load = [load(slope.at[j], slope_entry[j], 7 + j) for j in range(blocks)]
    low_load, unit1, mixed_load = load(saved.at[4], 6, 11), load(unit.at[0], 5, 12), load(saved.at[3], 4, 13)
    query_load, key_load, value_load = (load(saved.at[i], (2, 3, 6)[i], 14 + i) for i in range(3))
    x_load = load(x, 4, 17)
    down_fetch = [fetch(down_block(j), 0, 2 * j) for j in range(blocks)]
    up_fetch = [fetch(up_block(j), 1, 2 * j + 1) for j in range(blocks)]
    last = 2 * blocks
    output_fetch, query_fetch, key_fetch, value_fetch = (
        fetch(m, slot, last + i) for i, (m, slot) in enumerate(((3, 0), (0, 1), (1, 0), (2, 1)))
    )
    for copy in (unit2, own_load, across_load, act_load[0], down_fetch[0], up_fetch[0], slope_load[0], low_load):
        copy.start()
    to_sibling.start()
    here.start()
    total[0] = jnp.zeros_like(total[0])

    def folded(block):
        return jnp.sum(block.reshape(-1, 8, block.shape[-1]), axis=0)

    def norm_back(gain_row, shift_row, low_row, inverse, incoming, normed_entry, low_entry):
        def body(i, carry):
            spot = span(i, NORM_ROWS)
            grad, normed = incoming(spot), pool[normed_entry, spot].astype(f32)
            scaled = grad * small_full[gain_row : gain_row + 1, :]
            inner = (
                scaled
                - jnp.mean(scaled, axis=-1, keepdims=True)
                - normed * jnp.mean(scaled * normed, axis=-1, keepdims=True)
            )
            result = inner * inverse[spot]
            low = result.astype(bf16)
            hidden[spot] = result
            pool[low_entry, spot] = low
            return tuple(c + folded(b) for c, b in zip(carry, (grad * normed, grad, low.astype(f32))))

        zero = jnp.zeros((8, width), f32)
        found = lax.fori_loop(0, all_rows // NORM_ROWS, body, (zero, zero, zero))
        for row, value in zip((gain_row, shift_row, low_row), found):
            total[0, row : row + 1, :] = jnp.sum(value, axis=0, keepdims=True)

    def turned(slot):
        for y in range(2):
            yield pl.ds(y * width // 2, width // 2), weight[slot, y].reshape(width // 2, width)

    def own_half(slot):
        return term[slot, :, at.core]

    def half(i, m, left, right):
        core = lax.rem(at.core + 1 + i, 2)
        for y in range(2):
            picked = span(y * 2 + core, width // 4)
            value = down(pool[left, :, picked], pool[right]).astype(bf16)
            term[lax.rem(m, 2), y, core] = value.reshape(nz, nx, -1, width)
        pl.when(i == 0)(lambda: scatter.start(m, term.at[lax.rem(m, 2), :, 1 - at.core]))

    def run(code):
        kind, m = divmod(code, 100)
        if kind == 5:
            to_across(m).start()
        elif kind == 1:
            scatter.step1(m, own_half(m % 2))
        elif kind == 4:
            scatter.step4(m, out)
        else:
            (scatter.step2, scatter.step3)[kind - 2](m)

    def when(value, calls):
        for at_value, call in calls.items():
            pl.when(value == at_value)(partial(quietly, call))

    def load_second():
        for copy in (unit2, own_load, across_load):
            copy.wait()

    def second_norm():
        norm_back(6, 7, 5, inverse2, lambda spot: added(pool[2, spot], pool[3, spot]), 1, 0)
        act_load[1].start()
        act_load[2].start()

    def contract_term(i):
        j = i // 2
        middle = j * (3 - j) // 2
        when(i, {2 * n: act_load[n].wait for n in range(blocks)})
        half(lax.rem(i, 2), j, middle * (j + 1) + (1 - middle) * 5, 0)
        when(i, {1: act_load[3].start, 3: slope_load[1].start, 5: slope_load[2].start, 7: unit1.start})

    def widen_back(j):
        for n in range(blocks):
            when(j, {n: down_fetch[n].wait})
            when(j, {n: slope_load[n].wait})
        middle = j * (3 - j) // 2
        entry = middle * (j + 1) + (1 - middle) * 4
        for cols, part in turned(0):
            value = (across(pool[0], part) * pool[entry, :, cols].astype(f32)).astype(bf16)
            pool[1, :, cols] = value
            total[0, pl.ds(8 + j, 1), cols] = jnp.sum(value.astype(f32), axis=0, keepdims=True)
        fetches = [*down_fetch[1:], output_fetch]
        when(j, {n: fetches[n].start for n in range(blocks)})
        when(j, {0: slope_load[3].start, 1: query_load.start, 2: key_load.start, 3: mixed_load.start})

    def narrow_back(j):
        when(j, {n: up_fetch[n].wait for n in range(blocks)})
        for cols, part in turned(1):
            hidden[:, cols] = hidden[:, cols] + across(pool[1], part)
        fetches = [*up_fetch[1:], query_fetch]
        when(j, {n: fetches[n].start for n in range(blocks)})
        when(j, {blocks - 1: value_load.start})

    def feed_back(i):
        j, kind = i // 4, lax.rem(i, 4)
        when(i, {1: low_load.wait})
        pl.when(kind == 0)(lambda: widen_back(j))
        pl.when((kind == 1) | (kind == 2))(lambda: half(kind - 1, blocks + j, 6, 1))
        pl.when(kind == 3)(lambda: narrow_back(j))

    def first_norm():
        unit1.wait()
        norm_back(3, 4, 2, inverse1, lambda spot: hidden[spot], 5, 0)

    def mixed_back():
        output_fetch.wait()
        for cols, part in turned(0):
            pool[1, :, cols] = across(pool[0], part).astype(bf16)
        key_fetch.start()
        for copy in (query_load, key_load, value_load):
            copy.wait()
        fetch_probs(0).start()

    def output_term(i):
        when(i, {0: mixed_load.wait})
        half(i, jnp.int32(2 * blocks), 4, 0)
        when(i, {1: x_load.start})

    pairs = width // head_pair
    masks = half_masks(head_pair)
    scale = (head_pair // 2) ** (-0.5)

    def fetch_probs(i):
        slot = lax.rem(i, 2)
        return pltpu.make_async_copy(probs.at[i], held_probs.at[slot], ksem.at[slot])

    rounds = rows * pairs // 2

    def attend(i):
        pl.when(i + 1 < rounds)(lambda: fetch_probs(i + 1).start())
        fetch_probs(i).wait()
        spot, base = span(i // (pairs // 2), tokens), lax.rem(i, pairs // 2) * 2
        for p in range(2):
            cols = span(base + p, head_pair)
            query, keys, values, mixed_grad = (pool[e, spot, cols] for e in (2, 3, 6, 1))
            query_grad = key_grad = value_grad = None
            for h, mask in enumerate(masks):
                own_keys = keys * (mask * jnp.asarray(scale, bf16))
                low = held_probs[lax.rem(i, 2), 2 * p + h]
                prob = low.astype(f32)
                prob_grad = across(values * mask, mixed_grad)
                weighed = prob * prob_grad
                score_grad = (weighed - prob * jnp.sum(weighed, axis=0, keepdims=True)).astype(bf16)
                terms = (
                    down(score_grad, own_keys),
                    dot(score_grad, query * mask),
                    dot(low, mixed_grad * mask),
                )
                if query_grad is None:
                    query_grad, key_grad, value_grad = terms
                else:
                    query_grad, key_grad, value_grad = query_grad + terms[0], key_grad + terms[1], value_grad + terms[2]
            query_grad, value_grad = query_grad.astype(bf16), value_grad.astype(bf16)
            pool[2, spot, cols] = query_grad
            pool[3, spot, cols] = (key_grad * scale).astype(bf16)
            pool[6, spot, cols] = value_grad
            for row, value in ((0, query_grad), (1, value_grad)):
                found = jnp.sum(value.astype(f32), axis=0, keepdims=True)
                total[0, row : row + 1, cols] = total[0, row : row + 1, cols] + found

    def projection_term(i):
        n = i // 2
        later = (n + 1) // 2
        when(i, {0: x_load.wait})
        when(i, {0: sums.start})
        half(lax.rem(i, 2), 2 * blocks + 1 + n, 4, later * (n + 1) + (1 - later) * 6)
        when(i, {2 * n + 1: partial(sums.step, n) for n in range(3)})

    def pass_rows():
        for i in range(pieces):
            to_across(i).wait_recv()
        pass_on.start()

    done = pltpu.make_async_copy(hidden, input_out, hsem)

    def input_back(i):
        when(i, {0: query_fetch.wait, 1: key_fetch.wait, 2: value_fetch.wait})
        for cols, part in turned(lax.rem(i + 1, 2)):
            hidden[:, cols] = hidden[:, cols] + across(pool[2 + i + i // 2 * 2], part)
        when(i, {0: value_fetch.start, 1: pass_rows, 2: done.start})

    items = [load_second, second_norm, (2 * blocks, contract_term), (4 * blocks, feed_back), first_norm]
    items += [(2, output_term), mixed_back, (rounds, attend), (6, projection_term), (3, input_back)]
    drive(BACKWARD_ORDER, items, run)
    sums.finish(small_out)
    done.wait()

    for m in range(count):
        scatter.drain(m)
    here.wait()
    to_sibling.wait()
    for i in range(pieces):
        to_across(i).wait_send()
    pass_on.wait()


def backward(
    x, own_up, across_up, final, unit, inverse1, inverse2, small_full, act, slope, saved, g, probs, nz, nx, tokens
):
    f32, bf16 = jnp.float32, jnp.bfloat16
    count, _, _, _, _, shard_rows, width = g.shape
    acts = x.shape
    parts = [column_parts(width, s) for s in SCATTER_SHARES]
    vmem, anywhere = pl.BlockSpec(memory_space=pltpu.VMEM), pl.BlockSpec(memory_space=pl.ANY)
    dma = pltpu.SemaphoreType.DMA
    out = jax.ShapeDtypeStruct
    block = (2, 2, nz, nx, shard_rows, width)
    return pl.pallas_call(
        partial(backward_kernel, nz, nx, parts, tokens, 2 * width // HEADS),
        out_shape=[
            out((count, shard_rows, width), f32),
            out(small_full.shape, f32),
            out(acts, f32),
            out((2, 2, *acts), bf16),
        ],
        in_specs=[anywhere] * 5 + [vmem] * 3 + [anywhere] * 5,
        out_specs=[vmem, vmem, anywhere, anywhere],
        scratch_shapes=[
            *scatter_scratch(count, nz, nx, shard_rows, width, parts),
            *small_scratch(nz, small_full.shape),
            pltpu.VMEM((2, *block), bf16),
            pltpu.VMEM((2, *block), bf16),
            pltpu.VMEM((7, *acts), bf16),
            pltpu.VMEM(acts, f32),
            dma((count,)),
            dma((18,)),
            dma,
            dma((2,)),
            dma((2,)),
            dma((count,)),
            dma((count,)),
            dma,
            pltpu.VMEM((2, 4, tokens, tokens), bf16),
            dma((2,)),
        ],
        compiler_params=pltpu.CompilerParams(
            collective_id=2, has_side_effects=True, vmem_limit_bytes=63 * 2**20
        ),
    )(x, own_up, across_up, final, unit, inverse1, inverse2, small_full, act, slope, saved, g, probs)


def finish_kernel(
    slot_row, live_count, me, first, second, full, sums, small_sums,
    slot_acts, input_grad, query, keys, values, output, up, contract, *small,
):
    s = pl.program_id(0)
    slot_acts[0] = first[0]
    slot_acts[1] = second[0]
    input_grad[...] = jnp.where(s < live_count[0], full[...], 0.0)

    @pl.when(s == 0)
    def _():
        blocks = (sums.shape[0] - 4) // 2
        shard, width = query.shape
        for j in range(blocks):
            contract[j * shard : (j + 1) * shard, :] = sums[j]
        lanes = 128
        per = lanes // shard
        for q in range(width // lanes):
            part = [sums[blocks + j, :, q * lanes : (q + 1) * lanes] for j in range(blocks)]
            for t in range(per):
                found = jnp.concatenate([p[:, t * shard : (t + 1) * shard] for p in part], axis=1)
                at = (q * per + t) * blocks * shard
                up[:, at : at + blocks * shard] = found
        for i, ref in enumerate((output, values, query, keys)):
            ref[...] = sums[2 * blocks + i]
        own = pltpu.roll(small_sums[...], width - me[0] * shard, 1)
        for i in range(8):
            small[i][...] = own[i, :shard]
        small[8][...] = jnp.concatenate([own[8 + j : 9 + j, :shard] for j in range(blocks)], axis=1)[0]


def finish(slot_row, live_count, table, full, sums, small_sums):
    f32 = jnp.float32
    members, tokens, width = table.shape
    slots, rows = slot_row.shape[0], full.shape[0]
    assert slots == 2 * rows
    count, shard, _ = sums.shape
    blocks = (count - 4) // 2
    me = lax.axis_index(("dp", "fsdp")).astype(jnp.int32).reshape(1)
    block, pair = (1, tokens, width), (2, tokens, width)

    def fixed(shape):
        return pl.BlockSpec(shape, lambda s, *_: (0,) * len(shape))

    fixed_outs = [(shard, width)] * 4 + [(shard, blocks * width), (blocks * shard, width)]
    fixed_outs += [(shard,)] * 8 + [(blocks * shard,)]
    row = pl.BlockSpec(block, lambda s, *_: (s, 0, 0))

    def chosen(i):
        return pl.BlockSpec(block, lambda s, slot_row, *_: (jnp.clip(slot_row[2 * s + i], 0, members - 1), 0, 0))

    out = jax.ShapeDtypeStruct
    return pl.pallas_call(
        finish_kernel,
        out_shape=[
            out((slots, tokens, width), table.dtype),
            out(full.shape, f32),
            *(out(shape, f32) for shape in fixed_outs),
        ],
        grid_spec=pltpu.PrefetchScalarGridSpec(
            num_scalar_prefetch=3,
            grid=(rows,),
            in_specs=[
                chosen(0),
                chosen(1),
                row,
                fixed(sums.shape),
                fixed(small_sums.shape),
            ],
            out_specs=[
                pl.BlockSpec(pair, lambda s, *_: (s, 0, 0)),
                row,
                *(fixed(shape) for shape in fixed_outs),
            ],
        ),
        compiler_params=pltpu.CompilerParams(vmem_limit_bytes=63 * 2**20),
    )(slot_row, live_count, me, table, table, full, sums, small_sums)


def on_device_kernels(
    rows_in,
    slot_row,
    live_count,
    slot_activation_gradient,
    query_weight,
    key_weight,
    value_weight,
    output_weight,
    query_bias,
    value_bias,
    output_bias,
    attn_gain,
    attn_shift,
    expand_weight,
    up_bias,
    down_weight,
    down_bias,
    ffn_gain,
    ffn_shift,
):
    row_count, token_count, width = rows_in.shape
    nx = 2
    nz = lax.axis_size("fsdp") // nx
    small = [query_bias, value_bias, output_bias, attn_gain, attn_shift, down_bias, ffn_gain, ffn_shift, up_bias]
    x = rows_in.reshape(-1, width)
    g, probs, saved, act, slope, unit, final, own_up, across_up, small_full, inverse1, inverse2 = forward(
        x,
        [query_weight, key_weight, value_weight, output_weight],
        expand_weight,
        down_weight,
        small,
        slot_row,
        slot_activation_gradient,
        nz,
        nx,
        token_count,
    )
    sums, small_sums, input_full, table = backward(
        x,
        own_up,
        across_up,
        final,
        unit,
        inverse1,
        inverse2,
        small_full,
        act,
        slope,
        saved,
        g,
        probs,
        nz,
        nx,
        token_count,
    )
    slot_acts, input_grad, query, keys, values, output, up, contract, *small_grads = finish(
        slot_row,
        live_count,
        table.reshape(-1, token_count, width),
        input_full.reshape(rows_in.shape),
        sums,
        small_sums,
    )
    return (
        slot_acts,
        input_grad,
        query,
        keys,
        values,
        output,
        *small_grads[:5],
        up,
        small_grads[8],
        contract,
        *small_grads[5:8],
    )


def norm_forward(hidden, gain, shift):
    center = hidden - jnp.mean(hidden, axis=-1, keepdims=True)
    inverse = lax.rsqrt(jnp.mean(center * center, axis=-1, keepdims=True) + EPSILON)
    normed = center * inverse
    return (normed * gain + shift, normed, inverse)


def norm_backward(incoming, gain, normed, inverse):
    scaled = incoming * gain
    inner = (
        scaled
        - jnp.mean(scaled, axis=-1, keepdims=True)
        - normed * jnp.mean(scaled * normed, axis=-1, keepdims=True)
    )
    return (
        inner * inverse,
        jnp.sum(incoming * normed, axis=(0, 1)),
        jnp.sum(incoming, axis=(0, 1)),
    )


def apply_weight(acts, weight):
    return jnp.einsum("rsd,de->rse", acts, weight, preferred_element_type=jnp.float32)


def apply_back(grads, weight):
    return jnp.einsum("rse,de->rsd", grads, weight, preferred_element_type=jnp.float32)


def weight_term(acts, grads):
    return jnp.einsum("rsd,rse->de", acts, grads, preferred_element_type=jnp.float32)


def bias_term(grads):
    return jnp.sum(grads, axis=(0, 1), dtype=jnp.float32)


def on_device_plain(
    rows_in,
    slot_row,
    live_count,
    slot_activation_gradient,
    query_weight,
    key_weight,
    value_weight,
    output_weight,
    query_bias,
    value_bias,
    output_bias,
    attn_gain,
    attn_shift,
    expand_weight,
    up_bias,
    down_weight,
    down_bias,
    ffn_gain,
    ffn_shift,
):
    row_count, token_count, feature_count = rows_in.shape
    head_size = feature_count // HEADS
    score_scale = head_size ** (-0.5)
    split_shape = (row_count, token_count, HEADS, head_size)
    wanted = lax.broadcasted_iota(
        jnp.int32, (row_count * lax.axis_size("dp"), slot_row.shape[0]), 0
    )
    one_hot_matrix = (wanted == slot_row[None, :]).astype(jnp.bfloat16)
    upstream = lax.psum_scatter(
        jnp.einsum(
            "az,zfy->afy",
            one_hot_matrix,
            slot_activation_gradient,
            preferred_element_type=jnp.float32,
        ).astype(jnp.bfloat16),
        "dp",
        scatter_dimension=0,
        tiled=True,
    ).astype(jnp.float32)
    smalls = (query_bias, value_bias, output_bias, attn_gain, attn_shift, down_bias, ffn_gain, ffn_shift)
    small_rows = query_bias.shape[0]
    packed = jnp.concatenate([v.reshape(-1, small_rows) for v in (*smalls, up_bias)], axis=0)
    packed_full = lax.all_gather(packed, ("dp", "fsdp"), axis=0)
    (
        qbias_full,
        vbias_full,
        obias_full,
        gain1_full,
        shift1_full,
        downbias_full,
        gain2_full,
        shift2_full,
    ) = (packed_full[:, i].reshape(-1) for i in range(8))
    upbias_full = packed_full[:, 8:].reshape(-1)
    query_full, key_full, value_full, output_full, up_full, down_full = (
        lax.all_gather(weight, ("dp", "fsdp"), axis=0, tiled=True)
        for weight in (query_weight, key_weight, value_weight, output_weight, expand_weight, down_weight)
    )
    inputs = rows_in.astype(jnp.float32)
    query = (apply_weight(rows_in, query_full) + qbias_full.astype(jnp.float32)).astype(
        jnp.bfloat16
    )
    keys = apply_weight(rows_in, key_full).astype(jnp.bfloat16)
    values = (apply_weight(rows_in, value_full) + vbias_full.astype(jnp.float32)).astype(
        jnp.bfloat16
    )
    query_heads = query.reshape(split_shape)
    key_heads = keys.reshape(split_shape)
    value_heads = values.reshape(split_shape)
    scores = (
        jnp.einsum("rqhd,rkhd->rhqk", query_heads, key_heads, preferred_element_type=jnp.float32)
        * score_scale
    )
    row_top = jnp.max(scores, axis=-1, keepdims=True)
    expo = jnp.exp(scores - row_top)
    row_sum = jnp.sum(expo, axis=-1, keepdims=True)
    logsum = row_top + jnp.log(row_sum)
    probs_low = (expo / row_sum).astype(jnp.bfloat16)
    mixed = jnp.einsum(
        "rhqk,rkhd->rqhd", probs_low, value_heads, preferred_element_type=jnp.float32
    )
    mixed = mixed.reshape(row_count, token_count, feature_count).astype(jnp.bfloat16)
    gain1 = gain1_full.astype(jnp.float32)
    resid1 = inputs + apply_weight(mixed, output_full) + obias_full.astype(jnp.float32)
    normed1_out, normed1, inverse1 = norm_forward(resid1, gain1, shift1_full.astype(jnp.float32))
    normed1_low = normed1_out.astype(jnp.bfloat16)
    pre_act = apply_weight(normed1_low, up_full) + upbias_full.astype(jnp.float32)
    act_low = jax.nn.gelu(pre_act, approximate=False).astype(jnp.bfloat16)
    gain2 = gain2_full.astype(jnp.float32)
    resid2 = normed1_out + apply_weight(act_low, down_full) + downbias_full.astype(jnp.float32)
    final, second_normed, inverse2 = norm_forward(resid2, gain2, shift2_full.astype(jnp.float32))
    final_low = final.astype(jnp.bfloat16)
    shard_rows = lax.all_gather(final_low, "dp", axis=0, tiled=True)
    span_rows = shard_rows.shape[0]
    inside = (slot_row >= 0) & (slot_row < span_rows)
    picked = jnp.take(shard_rows, jnp.clip(slot_row, 0, span_rows - 1), axis=0)
    slot_acts = jnp.where(
        inside[:, None, None], picked, jnp.zeros(slot_activation_gradient.shape, jnp.bfloat16)
    )
    gain1 = gain1_full.astype(jnp.float32)
    gain2 = gain2_full.astype(jnp.float32)
    grad2, gain2_grad, shift2_grad = norm_backward(upstream, gain2, second_normed, inverse2)
    ffn_low = grad2.astype(jnp.bfloat16)
    down_grad = weight_term(act_low, ffn_low)
    down_bias_grad = bias_term(ffn_low)
    act_grad = apply_back(ffn_low, down_full)
    gelu_value, gelu_back = jax.vjp(partial(jax.nn.gelu, approximate=False), pre_act)
    pre_grad = gelu_back(act_grad)[0].astype(jnp.bfloat16)
    up_grad = weight_term(normed1_low, pre_grad)
    up_bias_grad = bias_term(pre_grad)
    normed1_grad = grad2 + apply_back(pre_grad, up_full)
    grad1, gain1_grad, shift1_grad = norm_backward(normed1_grad, gain1, normed1, inverse1)
    attn_low = grad1.astype(jnp.bfloat16)
    output_grad = weight_term(mixed, attn_low)
    output_bias_grad = bias_term(attn_low)
    mixed_grad = apply_back(attn_low, output_full).astype(jnp.bfloat16).reshape(split_shape)
    scores_again = (
        jnp.einsum("rqhd,rkhd->rhqk", query_heads, key_heads, preferred_element_type=jnp.float32)
        * score_scale
    )
    probs = jnp.exp(scores_again - logsum)
    probs_again = probs.astype(jnp.bfloat16)
    value_grad = jnp.einsum(
        "rhqk,rqhd->rkhd", probs_again, mixed_grad, preferred_element_type=jnp.float32
    )
    value_grad = value_grad.astype(jnp.bfloat16).reshape(row_count, token_count, feature_count)
    prob_grad = jnp.einsum(
        "rqhd,rkhd->rhqk", mixed_grad, value_heads, preferred_element_type=jnp.float32
    )
    score_grad = (probs * (prob_grad - jnp.sum(probs * prob_grad, axis=-1, keepdims=True))).astype(
        jnp.bfloat16
    )
    query_grad = (
        jnp.einsum("rhqk,rkhd->rqhd", score_grad, key_heads, preferred_element_type=jnp.float32)
        * score_scale
    )
    query_grad = query_grad.astype(jnp.bfloat16).reshape(row_count, token_count, feature_count)
    key_grad = (
        jnp.einsum("rhqk,rqhd->rkhd", score_grad, query_heads, preferred_element_type=jnp.float32)
        * score_scale
    )
    key_grad = key_grad.astype(jnp.bfloat16).reshape(row_count, token_count, feature_count)
    query_wgrad = weight_term(rows_in, query_grad)
    key_wgrad = weight_term(rows_in, key_grad)
    value_wgrad = weight_term(rows_in, value_grad)
    query_bias_grad = bias_term(query_grad)
    value_bias_grad = bias_term(value_grad)
    input_full = (
        grad1
        + apply_back(query_grad, query_full)
        + apply_back(key_grad, key_full)
        + apply_back(value_grad, value_full)
    )
    live_rows = lax.broadcasted_iota(jnp.int32, (row_count,), 0) < live_count[0]
    input_grad = jnp.where(live_rows[:, None, None], input_full, 0.0)
    devices = packed_full.shape[0]
    small_terms = jnp.concatenate(
        [
            v.reshape(devices, -1, small_rows)
            for v in (
                query_bias_grad,
                value_bias_grad,
                output_bias_grad,
                gain1_grad,
                shift1_grad,
                down_bias_grad,
                gain2_grad,
                shift2_grad,
                up_bias_grad,
            )
        ],
        axis=1,
    )
    small_sum = lax.psum_scatter(small_terms, ("dp", "fsdp"), scatter_dimension=0, tiled=True)[0]
    down_sum, up_sum, output_sum, value_sum, query_sum, key_sum = (
        lax.psum_scatter(
            term.astype(jnp.bfloat16), ("dp", "fsdp"), scatter_dimension=0, tiled=True
        ).astype(jnp.float32)
        for term in (down_grad, up_grad, output_grad, value_wgrad, query_wgrad, key_wgrad)
    )
    return (
        slot_acts,
        input_grad,
        query_sum,
        key_sum,
        value_sum,
        output_sum,
        small_sum[0],
        small_sum[1],
        small_sum[2],
        small_sum[3],
        small_sum[4],
        up_sum,
        small_sum[8:].reshape(-1),
        down_sum,
        small_sum[5],
        small_sum[6],
        small_sum[7],
    )


def solution(mesh):
    placed = (
        P(("dp", "fsdp"), None, None),
        P(("dp", "fsdp")),
        P(("dp", "fsdp")),
        P(("dp", "fsdp"), None, None),
        P(("dp", "fsdp"), None),
        P(("dp", "fsdp"), None),
        P(("dp", "fsdp"), None),
        P(("dp", "fsdp"), None),
        P(("dp", "fsdp")),
        P(("dp", "fsdp")),
        P(("dp", "fsdp")),
        P(("dp", "fsdp")),
        P(("dp", "fsdp")),
        P(("dp", "fsdp"), None),
        P(("dp", "fsdp")),
        P(("dp", "fsdp"), None),
        P(("dp", "fsdp")),
        P(("dp", "fsdp")),
        P(("dp", "fsdp")),
    )
    kernels = mesh.shape["dp"] == 4 and mesh.shape["fsdp"] == 8
    return jax.shard_map(
        on_device_kernels if kernels else on_device_plain,
        mesh=mesh,
        in_specs=placed,
        out_specs=(
            P(("dp", "fsdp"), None, None),
            P(("dp", "fsdp"), None, None),
            P(("dp", "fsdp"), None),
            P(("dp", "fsdp"), None),
            P(("dp", "fsdp"), None),
            P(("dp", "fsdp"), None),
            P(("dp", "fsdp")),
            P(("dp", "fsdp")),
            P(("dp", "fsdp")),
            P(("dp", "fsdp")),
            P(("dp", "fsdp")),
            P(("dp", "fsdp"), None),
            P(("dp", "fsdp")),
            P(("dp", "fsdp"), None),
            P(("dp", "fsdp")),
            P(("dp", "fsdp")),
            P(("dp", "fsdp")),
        ),
        check_vma=False,
    )
```

profile of v0, /device:TPU:0, one launch (start us, length us, event | category | flops | bytes accessed | tf_op | source)
XLA Modules:
  0.0 298.9 jit_solution(8516763987206083510)
XLA Ops:
  0.7 141.9 %shard_map.314 = (bf16[12,2,2,4,2,32,1024]{6,5,4,3,2,1,0:T(8,128)(2,1)}, bf16[12,4,320,320]{3,2,1,0:T(8,128)(2,1)}, bf16[5,960,1024]{2,1,0:T(8,128)(2,1)}, bf16[...) custom-call(bf16[960,1024]{1,0:T(8,128)(2,1)} %bitcast.6, ...), custom_call_target="tpu_custom_call" | custom-call | tf_op jit(solution)/shard_map/pallas_call | solution.py:697
  142.6 145.7 %shard_map.315 = (f32[12,32,1024]{2,1,0:T(8,128)}, f32[16,1024]{1,0:T(8,128)}, f32[960,1024]{1,0:T(8,128)}, bf16[2,2,960,1024]{3,2,1,0:T(8,128)(2,1)}) custom-call(bf16[960,1024]{1,0:T(8,128)(2,1)} %bitcast.7, bf16[960,1024]{1,0:T(8,128)(2,1)} %get-tuple-element.50.own_up, bf16[960,1024]{1,0:T(8,128)(2,1)} %get-tuple-element.51.across_up, ...), custom_call_target="tpu_custom_call" | custom-call | tf_op jit(solution)/shard_map/pallas_call | solution.py:1011
  289.0 9.7 %shard_map.316 = (bf16[6,320,1024]{2,1,0:T(8,128)(2,1)}, f32[3,320,1024]{2,1,0:T(8,128)}, f32[32,1024]{1,0:T(8,128)}, f32[32,1024]{1,0:T(8,128)}, f32[32,1024]{1...) custom-call(s32[6]{0:T(128)} %slot_row.3, ...), custom_call_target="tpu_custom_call" | custom-call | tf_op jit(solution)/shard_map/pallas_call | solution.py:1097
where the time goes:
time: 299 us
  Pallas kernels  297 us (99%)
    pallas_call x1, Pallas kernels, backward(): pl.pallas_call(partial(backward_kernel, nz, nx, parts, tokens, 2 * width...  146 us
    pallas_call x1, Pallas kernels, forward(): pl.pallas_call(partial(forward_kernel, nz, nx, [column_parts(width, s) fo...  142 us
    pallas_call x1, Pallas kernels, finish(): pl.pallas_call(finish_kernel, out_shape=[out((slots, tokens, width), tabl...  9.71 us

commit v1 on v0

--- a/solution.py
+++ b/solution.py
@@ -420,7 +420,6 @@
     all_rows, width = x.shape
     rows = all_rows // tokens
     at = Partners(nz, nx)
-    at.meet()
     gather = Gather(at, parts, count, shards, g, send, recv)
     sums = SmallSum(at, total, landing, ssend, srecv)
     groups = slots.shape[0] // rows
@@ -436,11 +435,12 @@
     own += [jnp.zeros((1, shard), f32)] * (total.shape[1] - len(own))
     own = jnp.concatenate(own, axis=0)
     total[0] = jnp.where(mine, jnp.concatenate([own] * (width // shard), axis=1), 0.0)
-    sums.start()
     for m in range(4):
         shards[m] = attention_weights[m][...]
     for i in range(slots.shape[0]):
         fetch(i).start()
+    at.meet()
+    sums.start()
 
     high, part = 32, width // 2
 
@@ -758,7 +758,6 @@
     all_rows, width = x.shape
     rows = all_rows // tokens
     at = Partners(nz, nx)
-    at.meet()
     scatter = Scatter(at, parts, rc, r3a, r3b, r2, rz, rcz, rcx, rcy, send, recv)
     sums = SmallSum(at, total, landing, ssend, srecv)
 
@@ -798,9 +797,10 @@
     )
     for copy in (unit2, own_load, across_load, act_load[0], down_fetch[0], up_fetch[0], slope_load[0], low_load):
         copy.start()
-    to_sibling.start()
     here.start()
     total[0] = jnp.zeros_like(total[0])
+    at.meet()
+    to_sibling.start()
 
     def folded(block):
         return jnp.sum(block.reshape(-1, 8, block.shape[-1]), axis=0)

time: 299 us -> 298 us (level)
  no operation moved by 1% of the time
where the time goes in v1:
time: 298 us
  Pallas kernels  296 us (99%)
    pallas_call x1, Pallas kernels, backward(): pl.pallas_call(partial(backward_kernel, nz, nx, parts, tokens, 2 * width...  145 us
    pallas_call x1, Pallas kernels, forward(): pl.pallas_call(partial(forward_kernel, nz, nx, [column_parts(width, s) fo...  142 us
    pallas_call x1, Pallas kernels, finish(): pl.pallas_call(finish_kernel, out_shape=[out((slots, tokens, width), tabl...  9.16 us

profile of v1, /device:TPU:0, one launch (start us, length us, event | category | flops | bytes accessed | tf_op | source)
XLA Modules:
  0.0 297.6 jit_solution(13056296866787051470)
XLA Ops:
  0.7 142.0 %shard_map.314 = (bf16[12,2,2,4,2,32,1024]{6,5,4,3,2,1,0:T(8,128)(2,1)}, bf16[12,4,320,320]{3,2,1,0:T(8,128)(2,1)}, bf16[5,960,1024]{2,1,0:T(8,128)(2,1)}, bf16[...) custom-call(bf16[960,1024]{1,0:T(8,128)(2,1)} %bitcast.6, ...), custom_call_target="tpu_custom_call" | custom-call | tf_op jit(solution)/shard_map/pallas_call | solution.py:697
  142.7 144.9 %shard_map.315 = (f32[12,32,1024]{2,1,0:T(8,128)}, f32[16,1024]{1,0:T(8,128)}, f32[960,1024]{1,0:T(8,128)}, bf16[2,2,960,1024]{3,2,1,0:T(8,128)(2,1)}) custom-call(bf16[960,1024]{1,0:T(8,128)(2,1)} %bitcast.7, bf16[960,1024]{1,0:T(8,128)(2,1)} %get-tuple-element.50.own_up, bf16[960,1024]{1,0:T(8,128)(2,1)} %get-tuple-element.51.across_up, ...), custom_call_target="tpu_custom_call" | custom-call | tf_op jit(solution)/shard_map/pallas_call | solution.py:1011
  288.2 9.2 %shard_map.316 = (bf16[6,320,1024]{2,1,0:T(8,128)(2,1)}, f32[3,320,1024]{2,1,0:T(8,128)}, f32[32,1024]{1,0:T(8,128)}, f32[32,1024]{1,0:T(8,128)}, f32[32,1024]{1...) custom-call(s32[6]{0:T(128)} %slot_row.3, ...), custom_call_target="tpu_custom_call" | custom-call | tf_op jit(solution)/shard_map/pallas_call | solution.py:1097
